TPU v7x, 32 devices: a whole 2x2x4 slice. The times are simulated.
32 devices in a mesh: seq: 8 (over z, y), head: 4 (over x, core).
Axes of the slice: x: 2, y: 2, z: 4, core: 2. Of those that a mesh axis runs over, the one named last changes fastest.
Arguments:
- vision: bfloat16 [16384, 7680], P(('seq', 'head')), may hold values from -6 to 6
- w_key: bfloat16 [7680, 512], replicated, may hold values from -0.0625 to 0.0625
- w_value: bfloat16 [7680, 512], replicated, may hold values from -0.0625 to 0.0625
- queries: bfloat16 [256, 4096], P('seq', 'head'), may hold values from -240 to 240
- w_out: bfloat16 [4096, 8192], P('head', 'seq'), may hold values from -0.09375 to 0.09375
Outputs:
- mixed: bfloat16 [256, 8192], P('head', 'seq')
All inputs are finite; a program needn't handle non-finite values.
Results may differ from a plain program's by a relative error of at most 0.03.
Values may be sent and summed in bfloat16 or wider, within the bound.
A program may use at most 128 MiB of HBM per device.

v0:
```python
import jax
import jax.numpy as jnp
from jax import lax
from jax.sharding import PartitionSpec as P

HD = 128


def scale_rows(partial_value, factor):
    return (
        partial_value.reshape(factor.shape[0], factor.shape[1], -1) * factor[:, :, None]
    ).reshape(factor.shape[0], -1)


def divide_rows(partial_value, denom):
    return (partial_value.reshape(denom.shape[0], denom.shape[1], -1) / denom[:, :, None]).reshape(
        denom.shape[0], -1
    )


def attend(queries_all, keys_here, values_here):
    head_size = HD
    kv_local = keys_here.shape[1] // head_size
    text_rows = queries_all.shape[0]
    q_heads = queries_all.shape[1] // head_size
    group_size = q_heads // kv_local
    grouped = queries_all.reshape(text_rows, kv_local, group_size, head_size)
    key_heads = keys_here.reshape(keys_here.shape[0], kv_local, head_size)
    value_heads = values_here.reshape(values_here.shape[0], kv_local, head_size)
    scores = jnp.einsum(
        "tkgd,nkd->kgtn", grouped, key_heads, preferred_element_type=jnp.float32
    ) * head_size ** (-0.5)
    maxima = jnp.max(scores, axis=-1)
    powers = jnp.exp(scores - maxima[..., None])
    totals = jnp.sum(powers, axis=-1)
    partial_value = jnp.einsum(
        "kgtn,nkd->tkgd",
        powers.astype(jnp.bfloat16),
        value_heads,
        preferred_element_type=jnp.float32,
    )
    partial_value = partial_value.reshape(text_rows, q_heads * head_size)
    maxima = maxima.transpose(2, 0, 1).reshape(text_rows, q_heads)
    totals = totals.transpose(2, 0, 1).reshape(text_rows, q_heads)
    return (maxima, totals, partial_value)


def shards(vision, w_key, w_value, queries, w_out):
    keys = jnp.dot(vision, w_key, preferred_element_type=jnp.float32).astype(jnp.bfloat16)
    values = jnp.dot(vision, w_value, preferred_element_type=jnp.float32).astype(jnp.bfloat16)
    keys_here, values_here = (
        lax.all_to_all(keys, "head", split_axis=1, concat_axis=0, tiled=True),
        lax.all_to_all(values, "head", split_axis=1, concat_axis=0, tiled=True),
    )
    queries_all = lax.all_gather(queries, "seq", axis=0, tiled=True)
    maxima, totals, partial_value = attend(queries_all, keys_here, values_here)
    global_max = lax.pmax(maxima, "seq")
    factor = jnp.exp(maxima - global_max)
    denom, numer = (
        lax.psum((totals * factor).astype(jnp.bfloat16), "seq").astype(jnp.float32),
        lax.psum(scale_rows(partial_value, factor).astype(jnp.bfloat16), "seq").astype(jnp.float32),
    )
    attended = divide_rows(numer, denom).astype(jnp.bfloat16)
    return lax.psum_scatter(
        jnp.dot(attended, w_out, preferred_element_type=jnp.float32).astype(jnp.bfloat16),
        "head",
        scatter_dimension=0,
        tiled=True,
    )


def solution(mesh):
    placed = (P(("seq", "head"), None), P(), P(), P("seq", "head"), P("head", "seq"))
    return jax.shard_map(
        shards, mesh=mesh, in_specs=placed, out_specs=P("head", "seq"), check_vma=False
    )
```

profile of v0, /device:TPU:0, one launch (start us, length us, event | category | flops | bytes accessed | tf_op | source)
XLA Modules:
  0.0 224.4 jit_solution(7938568385379473497)
XLA Ops:
  6.5 0.0 copy-start
  6.5 10.7 %convolution_convert_fusion.1 = bf16[512,512]{0,1:T(8,128)(2,1)} fusion(bf16[512,7680]{1,0:T(8,128)(2,1)} %param.5, bf16[7680,512]{1,0:T(8,128)(2,1)} %param.7), kind=kOutput, calls=%fused_computation.8 | convolution fusion | flops 4026793984 | bytes 16252928 | tf_op jit(solution)/shard_map/dot_general | solution.py:50
  17.2 4.2 %all-to-all-start = ((bf16[512,4,128]{0,2,1:T(8,128)(2,1)}), bf16[512,4,128]{0,2,1:T(8,128)(2,1)S(1)}, u32[]{:S(2)}, u32[]{:S(2)}) async-start(bf16[512,4,128]{0,2,1:T(8,128)(2,1)} %bitcast), calls=%async_computation | async-start | bytes 1048576 | tf_op jit(solution)/shard_map/all_to_all | solution.py:53
  21.4 0.0 copy-start.2
  21.4 10.6 %convolution_convert_fusion = bf16[512,512]{0,1:T(8,128)(2,1)} fusion(bf16[512,7680]{1,0:T(8,128)(2,1)} %param.5, bf16[7680,512]{1,0:T(8,128)(2,1)} %param.6), kind=kOutput, calls=%fused_computation.7 | convolution fusion | flops 4026793984 | bytes 16252928 | tf_op jit(solution)/shard_map/dot_general | solution.py:49
  32.0 0.0 all-to-all-done
  32.0 4.1 %all-to-all-start.1 = ((bf16[512,4,128]{0,2,1:T(8,128)(2,1)}), bf16[512,4,128]{0,2,1:T(8,128)(2,1)}, u32[]{:S(2)}, u32[]{:S(2)}) async-start(bf16[512,4,128]{0,2,1:T(8,128)(2,1)} %bitcast.2), calls=%async_computation.1 | async-start | bytes 1048576 | tf_op jit(solution)/shard_map/all_to_all | solution.py:52
  36.1 0.0 all-reduce.2.cloned.1.call-start
  36.2 0.0 copy-done.2
  36.2 34.5 %all_gather.3 = bf16[256,1024]{1,0:T(8,128)(2,1)} all-gather(bf16[32,1024]{1,0:T(8,128)(2,1)S(1)} %copy-done.2), channel_id=1, replica_groups=mesh['seq'=8,'head'=4] {'seq'}, dimensions={0}, use_global_device_ids=true | all-gather | bytes 589824 | tf_op jit(solution)/shard_map/all_gather | solution.py:55
  70.7 1.2 copy.16
  72.0 1.2 copy.14
  73.2 2.2 reshape.57
  75.4 0.0 all-to-all-done.1
  75.4 1.3 copy.15
  76.7 8.0 %bitcast_reduce_fusion = (f32[8,256]{1,0:T(8,128)S(1)}, f32[2048,256,8]{1,0,2:T(8,128)}) fusion(bf16[2048,128,1]{1,0,2:T(8,128)(2,1)S(1)} %bitcast.66, bf16[256,8,128]{0,2,1:T(8,128)(2,1)S(1)} %bitcast.65), kind=kOutput, calls=%fused_computation.1 | convolution fusion | flops 1082128384 | bytes 17833984 | tf_op jit(solution)/shard_map/tkgd,nkd->kgtn/dot_general | solution.py:30
  84.8 0.0 copy-start.1
  84.8 8.5 %fusion.1 = f32[8,256]{1,0:T(8,128)S(1)} fusion(f32[2048,256,8]{1,0,2:T(8,128)} %get-tuple-element.8, f32[8,256]{1,0:T(8,128)S(1)} %get-tuple-element.7), kind=kLoop, calls=%fused_computation.3 | loop fusion | flops 12580864 | bytes 16793600 | tf_op jit(solution)/shard_map/reduce_sum | solution.py:35
  93.3 0.0 copy-done.1
  93.3 7.4 %fusion.4 = f32[128,8,256]{2,0,1:T(8,128)S(1)} fusion(bf16[2048,128,1]{0,1,2:T(8,128)(2,1)S(1)} %copy-done.1, f32[2048,256,8]{1,0,2:T(8,128)} %get-tuple-element.8, f32[8,256]{1,0:T(8,128)S(1)} %get-tuple-element.7), kind=kOutput, calls=%fused_computation.6 | convolution fusion | flops 1086324736 | bytes 18358272 | tf_op jit(solution)/shard_map/kgtn,nkd->tkgd/dot_general | solution.py:36
  100.8 21.8 %pmax.7 = f32[256,8]{0,1:T(8,128)S(1)} all-reduce(f32[256,8]{0,1:T(8,128)S(1)} %bitcast.68), channel_id=1, replica_groups=mesh['seq'=8,'head'=4] {'seq'}, use_global_device_ids=true, to_apply=%region_1.0 | all-reduce | flops 2048 | bytes 16384 | tf_op jit(solution)/shard_map/pmax | solution.py:57
  122.5 0.9 fusion.6
  123.4 0.0 all-reduce.2.cloned.1.call-update
  123.5 0.0 reduce-scatter.2.cloned.1.call-start
  123.5 17.2 %psum.15 = bf16[256,8]{0,1:T(8,128)(2,1)S(1)} all-reduce(bf16[256,8]{0,1:T(8,128)(2,1)S(1)} %get-tuple-element.5), channel_id=1, replica_groups=mesh['seq'=8,'head'=4] {'seq'}, use_global_device_ids=true, to_apply=%region_4.0 | all-reduce | flops 2048 | bytes 8192 | tf_op jit(solution)/shard_map/psum | solution.py:60
  140.7 53.1 %all-reduce.2.cloned.1.call-done = bf16[256,1024]{0,1:T(8,128)(2,1)} async-done(((bf16[256,1024]{0,1:T(8,128)(2,1)}), bf16[256,1024]{0,1:T(8,128)(2,1)}) %all-reduce.2.cloned.1.call-update) | async-done | bytes 524304 | tf_op jit(solution)/shard_map/psum | solution.py:61
  193.8 1.1 fusion.7
  194.9 0.0 copy-done
  194.9 1.5 convolution_convert_fusion.2
  196.5 0.0 reduce-scatter.2.cloned.1.call-update
  196.5 21.1 %reduce-scatter.2.cloned.1.call-done = bf16[64,1024]{1,0:T(8,128)(2,1)} async-done(((bf16[256,1024]{1,0:T(8,128)(2,1)}), bf16[64,1024]{1,0:T(8,128)(2,1)}) %reduce-scatter.2.cloned.1.call-update) | async-done | bytes 131088 | tf_op jit(solution)/shard_map/reduce_scatter | solution.py:64
  (2 shorter events, 0.0 us)
Async XLA Ops:
  6.5 188.4 %copy-start = (bf16[1024,1024]{1,0:T(8,128)(2,1)S(1)}, bf16[1024,1024]{1,0:T(8,128)(2,1)}, u32[]{:S(2)}) copy-start(bf16[1024,1024]{1,0:T(8,128)(2,1)} %param.9) | copy-start | bytes 6291460
  17.2 14.8 %all-to-all-start = ((bf16[512,4,128]{0,2,1:T(8,128)(2,1)}), bf16[512,4,128]{0,2,1:T(8,128)(2,1)S(1)}, u32[]{:S(2)}, u32[]{:S(2)}) async-start(bf16[512,4,128]{0,2,1:T(8,128)(2,1)} %bitcast), calls=%async_computation | async-start | bytes 1048576 | tf_op jit(solution)/shard_map/all_to_all | solution.py:53
  21.4 14.8 %copy-start.2 = (bf16[32,1024]{1,0:T(8,128)(2,1)S(1)}, bf16[32,1024]{1,0:T(8,128)(2,1)}, u32[]{:S(2)}) copy-start(bf16[32,1024]{1,0:T(8,128)(2,1)} %param.8) | copy-start | bytes 196612
  32.0 43.4 %all-to-all-start.1 = ((bf16[512,4,128]{0,2,1:T(8,128)(2,1)}), bf16[512,4,128]{0,2,1:T(8,128)(2,1)}, u32[]{:S(2)}, u32[]{:S(2)}) async-start(bf16[512,4,128]{0,2,1:T(8,128)(2,1)} %bitcast.2), calls=%async_computation.1 | async-start | bytes 1048576 | tf_op jit(solution)/shard_map/all_to_all | solution.py:52
  36.1 157.7 %all-reduce.2.cloned.1.call-start = ((), (), s32[]{:S(2)}) async-start(), calls=%async_computation.3 | async-start | bytes 1048576 | tf_op jit(solution)/shard_map/psum | solution.py:61
  84.8 8.5 %copy-start.1 = (bf16[2048,128,1]{0,1,2:T(8,128)(2,1)S(1)}, bf16[2048,128,1]{0,1,2:T(8,128)(2,1)}, u32[]{:S(2)}) copy-start(bf16[2048,128,1]{0,1,2:T(8,128)(2,1)} %reshape.57) | copy-start | bytes 1572868
  123.5 94.1 %reduce-scatter.2.cloned.1.call-start = ((), (), s32[]{:S(2)}) async-start(), calls=%async_computation.4 | async-start | bytes 655360 | tf_op jit(solution)/shard_map/reduce_scatter | solution.py:64
Sparse Core Ops, SparseCore 0:
  123.6 70.1 all-reduce.1
  196.6 20.9 reduce-scatter.1
where the time goes:
time: 225 us; the launch traced here: 224 us
  waiting for transfers between devices  74.3 us (33%)
  blocking collectives  73.5 us (33%)
  matrix products  38.2 us (17%)
  between operations  13.5 us (6%)
  other arithmetic  10.6 us (5%)
  starting transfers between devices  8.43 us (4%)
  local copies, waits for them, and re-layouts  5.99 us (3%)
    psum x1, waiting for transfers between devices, shards(): lax.psum(scale_rows(partial_value, factor).astype(jnp.bfloat16), 'seq')  53.1 us
    all_gather x1, blocking collectives, shards(): queries_all = lax.all_gather(queries, 'seq', axis=0, tiled=True)  34.5 us
    pmax x1, blocking collectives, shards(): global_max = lax.pmax(maxima, 'seq')  21.8 us
    reduce_scatter x1, waiting for transfers between devices, shards(): lax.psum_scatter(jnp.dot(attended, w_out, preferred_element_type=jnp.floa...  21.1 us
    psum x1, blocking collectives, shards(): lax.psum((totals * factor).astype(jnp.bfloat16), 'seq').astype(jnp.float32)  17.2 us
    dot_general x1, matrix products, shards(): jnp.dot(vision, w_value, preferred_element_type=jnp.float32)  10.7 us
    dot_general x1, matrix products, shards(): jnp.dot(vision, w_key, preferred_element_type=jnp.float32)  10.6 us
    reduce_sum x1, other arithmetic, attend(): totals = jnp.sum(powers, axis=-1)  8.54 us
  transfers between devices with their start and end apart: 4, of which 2 were waited for; matrix products, arithmetic and copies ran while one was open for 7% of the time, Pallas kernels for 0%

commit v1 on v0

v1 whole, which is shorter than its diff:
```python
import functools
import math

import jax
import jax.numpy as jnp
from jax import lax
from jax.experimental import pallas as pl
from jax.experimental.pallas import tpu as pltpu
from jax.sharding import PartitionSpec as P

HD = 128
F32 = jnp.float32
BF16 = jnp.bfloat16
MESH = pl.DeviceIdType.MESH


def eye_mask(rows):
    return lax.broadcasted_iota(jnp.int32, (rows, HD), 0) == lax.broadcasted_iota(
        jnp.int32, (rows, HD), 1
    )


def to_rows(col, unit):
    part = min(unit, HD)
    eye = eye_mask(part)
    return [
        jnp.sum(jnp.where(eye, col[i * part : (i + 1) * part], 0.0), axis=0, keepdims=True)
        for i in range(unit // part)
    ]


def to_col(rows, unit):
    part = min(unit, HD)
    eye = eye_mask(part)
    parts = [
        jnp.sum(
            jnp.where(eye, jnp.broadcast_to(rows[i : i + 1], (part, HD)), 0.0),
            axis=1,
            keepdims=True,
        )
        for i in range(unit // part)
    ]
    return parts[0] if len(parts) == 1 else jnp.concatenate(parts, axis=0)


def kernel(
    n_s, n_h, n_c,
    vision, w_key, w_value, q, w_out, out,
    vbuf, wbuf, wobuf, acc, q_all, k_send, v_send, k_all, v_ext,
    o_near, m_near, o_send, s_send, o_recv, s_recv, a_send, a_full, r_send, r_recv,
    v_sem, wk_sem, wv_sem, wo_sem,
    q_ss, q_rs, k_ss, k_rs, vv_ss, vv_rs, o_ss, o_rs, s_ss, s_rs, a_ss, a_rs, r_ss, r_rs,
):
    me_s = lax.axis_index("seq")
    me_h = lax.axis_index("head")
    k_c = vbuf.shape[2]
    text_local = q.shape[0]
    heads = q.shape[1] // HD
    unit = text_local * heads
    per_head = n_s // heads
    half = n_h // 2
    n_rows = max(1, unit // HD)
    scale = math.log2(math.e) / math.sqrt(HD)

    def head_at(offset):
        return (lax.rem(me_h // 2 + offset // 2, half)) * 2 + lax.rem(
            lax.rem(me_h, 2) + lax.rem(offset, 2), 2
        )

    def head_from(offset):
        return (lax.rem(me_h // 2 + half - offset // 2, half)) * 2 + lax.rem(
            lax.rem(me_h, 2) + lax.rem(offset, 2), 2
        )

    def load_vision(c):
        return pltpu.make_async_copy(
            vision.at[:, pl.ds(pl.multiple_of(c * k_c, HD), k_c)], vbuf.at[c], v_sem.at[c]
        )

    def load_w(p, c):
        cols = pl.ds(pl.multiple_of(head_at(n_h - 1 - p) * HD, HD), HD)
        rows = pl.ds(pl.multiple_of(c * k_c, HD), k_c)
        return (
            pltpu.make_async_copy(
                w_key.at[rows, cols], wbuf.at[p, c, :, pl.ds(0, HD)], wk_sem.at[p, c]
            ),
            pltpu.make_async_copy(
                w_value.at[rows, cols], wbuf.at[p, c, :, pl.ds(HD, HD)], wv_sem.at[p, c]
            ),
        )

    def start_w(p, c):
        for copy in load_w(p, c):
            copy.start()

    def wait_w(p, c):
        for copy in load_w(p, c):
            copy.wait()

    def first_loads(c, carry):
        load_vision(c).start()
        start_w(0, c)
        return carry

    lax.fori_loop(0, n_c, first_loads, 0)

    barrier = pltpu.get_barrier_semaphore()

    def greet_seq(i, carry):
        pl.semaphore_signal(
            barrier, inc=1, device_id=(lax.rem(me_s + i, n_s), me_h), device_id_type=MESH
        )
        return carry

    def greet_head(i, carry):
        pl.semaphore_signal(
            barrier, inc=1, device_id=(me_s, lax.rem(me_h + i, n_h)), device_id_type=MESH
        )
        return carry

    lax.fori_loop(1, n_s, greet_seq, 0)
    lax.fori_loop(1, n_h, greet_head, 0)
    v_ext[:, :, HD:] = jnp.ones((n_h, v_ext.shape[1], HD), BF16)
    q_all[me_s] = q[...]
    pl.semaphore_wait(barrier, n_s + n_h - 2)

    def q_copy(to, slot, i):
        return pltpu.make_async_remote_copy(
            src_ref=q, dst_ref=q_all.at[slot], send_sem=q_ss.at[i], recv_sem=q_rs.at[i],
            device_id=(to, me_h), device_id_type=MESH,
        )

    def q_start(i, carry):
        q_copy(lax.rem(me_s + i, n_s), me_s, i).start()
        return carry

    lax.fori_loop(1, n_s, q_start, 0)

    def kv_copies(offset, to):
        return (
            pltpu.make_async_remote_copy(
                src_ref=k_send.at[offset], dst_ref=k_all.at[offset],
                send_sem=k_ss.at[offset], recv_sem=k_rs.at[offset],
                device_id=(me_s, to), device_id_type=MESH,
            ),
            pltpu.make_async_remote_copy(
                src_ref=v_send.at[offset], dst_ref=v_ext.at[offset, :, pl.ds(0, HD)],
                send_sem=vv_ss.at[offset], recv_sem=vv_rs.at[offset],
                device_id=(me_s, to), device_id_type=MESH,
            ),
        )

    for p in range(n_h):
        offset = n_h - 1 - p

        def chunk(c, carry, p=p):
            if p == 0:
                load_vision(c).wait()
            wait_w(p, c)
            if p + 1 < n_h:
                start_w(p + 1, c)
            got = jnp.dot(vbuf[c], wbuf[p, c], preferred_element_type=F32)

            @pl.when(c == 0)
            def _():
                acc[...] = got

            @pl.when(c > 0)
            def _():
                acc[...] += got

            return carry

        lax.fori_loop(0, n_c, chunk, 0)
        if offset:
            k_send[offset] = acc[:, :HD].astype(BF16)
            v_send[offset] = acc[:, HD:].astype(BF16)
            for copy in kv_copies(offset, head_at(offset)):
                copy.start()
        else:
            k_all[0] = acc[:, :HD].astype(BF16)
            v_ext[0, :, :HD] = acc[:, HD:].astype(BF16)

    load_out = pltpu.make_async_copy(w_out, wobuf, wo_sem)
    load_out.start()

    def q_wait(i, carry):
        q_copy(lax.rem(me_s + i, n_s), lax.rem(me_s + n_s - i, n_s), i).wait_recv()
        return carry

    lax.fori_loop(1, n_s, q_wait, 0)

    def block(u, first, last):
        col = pl.ds(pl.multiple_of((u // per_head) * HD, HD), HD)
        rows = pl.ds(0, heads) if per_head == 1 else pl.ds(lax.rem(u, per_head) * heads, heads)
        qv = q_all[rows, :, col].reshape(unit, HD)
        k = k_all[first:last].reshape(-1, HD)
        v = v_ext[first:last].reshape(-1, 2 * HD)
        s = lax.dot_general(qv, k, (((1,), (1,)), ((), ())), preferred_element_type=F32)
        m = jnp.max(s, axis=1, keepdims=True)
        w = jnp.exp2((s - m) * scale).astype(BF16)
        return jnp.dot(w, v, preferred_element_type=F32), jnp.broadcast_to(m, (unit, HD))

    for offset in range(1, half):
        for copy in kv_copies(offset, head_from(offset)):
            copy.wait_recv()

    def near(i, carry):
        o, m = block(lax.rem(me_s + 1 + i, n_s), 0, half)
        o_near[i] = o
        m_near[i] = m
        return carry

    lax.fori_loop(0, n_s, near, 0)

    for offset in range(half, n_h):
        for copy in kv_copies(offset, head_from(offset)):
            copy.wait_recv()

    def o_copies(i, to, slot):
        return (
            pltpu.make_async_remote_copy(
                src_ref=o_send.at[i], dst_ref=o_recv.at[slot],
                send_sem=o_ss.at[i], recv_sem=o_rs.at[i],
                device_id=(to, me_h), device_id_type=MESH,
            ),
            pltpu.make_async_remote_copy(
                src_ref=s_send.at[i], dst_ref=s_recv.at[slot],
                send_sem=s_ss.at[i], recv_sem=s_rs.at[i],
                device_id=(to, me_h), device_id_type=MESH,
            ),
        )

    def far_block(i, u):
        o2, m2 = block(u, half, n_h)
        o1, m1 = o_near[i], m_near[i]
        m = jnp.maximum(m1, m2)
        e1 = jnp.exp2((m1 - m) * scale)
        e2 = jnp.exp2((m2 - m) * scale)
        numer = o1[:, :HD] * e1 + o2[:, :HD] * e2
        total = o1[:, HD:] * e1 + o2[:, HD:] * e2
        return numer.astype(BF16), to_rows(m, unit), to_rows(total, unit)

    def far(i, carry):
        u = lax.rem(me_s + 1 + i, n_s)
        numer, m_rows, t_rows = far_block(i, u)
        o_send[i] = numer
        for r in range(n_rows):
            s_send[i, r : r + 1] = m_rows[r]
            s_send[i, n_rows + r : n_rows + r + 1] = t_rows[r]
        for copy in o_copies(i, u, me_s):
            copy.start()
        return carry

    lax.fori_loop(0, n_s - 1, far, 0)
    numer, m_rows, t_rows = far_block(n_s - 1, me_s)
    o_recv[me_s] = numer
    for r in range(n_rows):
        s_recv[me_s, r : r + 1] = m_rows[r]
        s_recv[me_s, n_rows + r : n_rows + r + 1] = t_rows[r]

    def o_wait(i, carry):
        for copy in o_copies(i, lax.rem(me_s + 1 + i, n_s), lax.rem(me_s + n_s - 1 - i, n_s)):
            copy.wait_recv()
        return carry

    lax.fori_loop(0, n_s - 1, o_wait, 0)
    m_all = s_recv[:, 0:n_rows]
    m_top = jnp.max(m_all, axis=0, keepdims=True)
    e_all = jnp.exp2((m_all - m_top) * scale)
    f_all = e_all / jnp.sum(e_all * s_recv[:, n_rows : 2 * n_rows], axis=0, keepdims=True)
    att = jnp.zeros((unit, HD), F32)
    for b in range(n_s):
        att += to_col(f_all[b], unit) * o_recv[b].astype(F32)
    a_send[...] = att.astype(BF16)

    def place(u):
        rows = (
            pl.ds(0, unit)
            if per_head == 1
            else pl.ds(pl.multiple_of(lax.rem(u, per_head) * unit, 16), unit)
        )
        return rows, pl.ds(pl.multiple_of((u // per_head) * HD, HD), HD)

    def a_copy(i, to, u):
        rows, cols = place(u)
        return pltpu.make_async_remote_copy(
            src_ref=a_send, dst_ref=a_full.at[rows, cols],
            send_sem=a_ss.at[i], recv_sem=a_rs.at[i],
            device_id=(to, me_h), device_id_type=MESH,
        )

    def a_start(i, carry):
        a_copy(i, lax.rem(me_s + i, n_s), me_s).start()
        return carry

    def a_wait(i, carry):
        a_copy(i, lax.rem(me_s + i, n_s), lax.rem(me_s + n_s - i, n_s)).wait_recv()
        return carry

    lax.fori_loop(1, n_s, a_start, 0)
    rows, cols = place(me_s)
    a_full[rows, cols] = a_send[...]
    load_out.wait()
    lax.fori_loop(1, n_s, a_wait, 0)

    share = jnp.dot(a_full[...], wobuf[...], preferred_element_type=F32)
    r_send[...] = share.astype(BF16).reshape(r_send.shape)

    def r_copy(offset, to):
        return pltpu.make_async_remote_copy(
            src_ref=r_send.at[to], dst_ref=r_recv.at[offset],
            send_sem=r_ss.at[offset], recv_sem=r_rs.at[offset],
            device_id=(me_s, to), device_id_type=MESH,
        )

    for offset in range(n_h - 1, 0, -1):
        r_copy(offset, head_at(offset)).start()
    total = r_send[me_h].astype(F32)
    for offset in range(1, n_h):
        r_copy(offset, head_from(offset)).wait_recv()
        total += r_recv[offset].astype(F32)
    out[...] = total.astype(BF16)

    def q_sent(i, carry):
        q_copy(lax.rem(me_s + i, n_s), me_s, i).wait_send()
        a_copy(i, lax.rem(me_s + i, n_s), me_s).wait_send()
        return carry

    def o_sent(i, carry):
        for copy in o_copies(i, lax.rem(me_s + 1 + i, n_s), me_s):
            copy.wait_send()
        return carry

    lax.fori_loop(1, n_s, q_sent, 0)
    lax.fori_loop(0, n_s - 1, o_sent, 0)
    for offset in range(1, n_h):
        for copy in kv_copies(offset, head_at(offset)):
            copy.wait_send()
        r_copy(offset, head_at(offset)).wait_send()


def shards(n_s, n_h, vision, w_key, w_value, queries, w_out):
    tokens, width = vision.shape
    text_local, features = queries.shape
    heads = features // HD
    text = text_local * n_s
    unit = text_local * heads
    out_cols = w_out.shape[1]
    n_c = max(d for d in range(1, 7) if width % (d * HD) == 0)
    k_c = width // n_c
    vmem = pltpu.VMEM
    dma = pltpu.SemaphoreType.DMA
    scratch = [
        vmem((n_c, tokens, k_c), BF16),
        vmem((n_h, n_c, k_c, 2 * HD), BF16),
        vmem(w_out.shape, BF16),
        vmem((tokens, 2 * HD), F32),
        vmem((n_s, text_local, features), BF16),
        vmem((n_h, tokens, HD), BF16),
        vmem((n_h, tokens, HD), BF16),
        vmem((n_h, tokens, HD), BF16),
        vmem((n_h, tokens, 2 * HD), BF16),
        vmem((n_s, unit, 2 * HD), F32),
        vmem((n_s, unit, HD), F32),
        vmem((n_s, unit, HD), BF16),
        vmem((n_s, 8, HD), F32),
        vmem((n_s, unit, HD), BF16),
        vmem((n_s, 8, HD), F32),
        vmem((unit, HD), BF16),
        vmem((text, features), BF16),
        vmem((n_h, text // n_h, out_cols), BF16),
        vmem((n_h, text // n_h, out_cols), BF16),
        dma((n_c,)), dma((n_h, n_c)), dma((n_h, n_c)), dma,
        dma((n_s,)), dma((n_s,)),
        dma((n_h,)), dma((n_h,)), dma((n_h,)), dma((n_h,)),
        dma((n_s,)), dma((n_s,)), dma((n_s,)), dma((n_s,)),
        dma((n_s,)), dma((n_s,)),
        dma((n_h,)), dma((n_h,)),
    ]
    anywhere = pl.BlockSpec(memory_space=pl.ANY)
    inside = pl.BlockSpec(memory_space=pltpu.VMEM)
    return pl.pallas_call(
        functools.partial(kernel, n_s, n_h, n_c),
        out_shape=jax.ShapeDtypeStruct((text // n_h, out_cols), BF16),
        in_specs=[anywhere, anywhere, anywhere, inside, anywhere],
        out_specs=inside,
        scratch_shapes=scratch,
        compiler_params=pltpu.CompilerParams(
            collective_id=0, has_side_effects=True, vmem_limit_bytes=56 * 1024 * 1024
        ),
    )(vision, w_key, w_value, queries, w_out)


def solution(mesh):
    placed = (P(("seq", "head"), None), P(), P(), P("seq", "head"), P("head", "seq"))
    return jax.shard_map(
        functools.partial(shards, mesh.shape["seq"], mesh.shape["head"]),
        mesh=mesh, in_specs=placed, out_specs=P("head", "seq"), check_vma=False,
    )
```

time: 225 us -> 66.4 us (0.30)
  the two profiles are of different devices: /device:TPU:0 before, /device:TPU:28 now
where the time goes in v1:
time: 66.4 us; the launch traced here: 66.2 us
  Pallas kernels  64.6 us (97%)
  local copies, waits for them, and re-layouts  1.57 us (2%)
    pallas_call x1, Pallas kernels, shards(): pl.pallas_call(functools.partial(kernel, n_s, n_h, n_c), out_shape=jax.Sh...  64.6 us
    unnamed x1, local copies, waits for them, and re-layouts  1.57 us

profile of v1, /device:TPU:28, one launch (start us, length us, event | category | flops | bytes accessed | tf_op | source)
XLA Modules:
  0.0 66.2 jit_solution(18195556970133673599)
XLA Ops:
  0.0 64.6 %shard_map.55 = bf16[64,1024]{1,0:T(8,128)(2,1)} custom-call(bf16[512,7680]{1,0:T(8,128)(2,1)} %vision.1, bf16[7680,512]{1,0:T(8,128)(2,1)} %w_key.1, bf16[7680,512]{1,0:T(8,128)(2,1)} %w_value.1, bf16[32,1024]{1,0:T(8,128)(2,1)} %q.1, bf16[1024,1024]{1,0:T(8,128)(2,1)} %w_out.1), custom_call_target="tpu_custom_call" | custom-call | tf_op jit(solution)/shard_map/pallas_call | solution.py:383
  64.6 1.6 %copy.7 = bf16[64,1024]{1,0:T(8,128)(2,1)} copy(bf16[64,1024]{1,0:T(8,128)(2,1)} %shard_map.55) | data formatting | bytes 262144

commit v2 on v1

--- a/solution.py
+++ b/solution.py
@@ -47,9 +47,10 @@
     n_s, n_h, n_c,
     vision, w_key, w_value, q, w_out, out,
     vbuf, wbuf, wobuf, acc, q_all, k_send, v_send, k_all, v_ext,
-    o_near, m_near, o_send, s_send, o_recv, s_recv, a_send, a_full, r_send, r_recv,
+    o_near, m_near, p_send, t_send, p_recv, t_recv, o_send, s_send, o_recv, s_recv, a_send, a_full, r_send, r_recv,
     v_sem, wk_sem, wv_sem, wo_sem,
-    q_ss, q_rs, k_ss, k_rs, vv_ss, vv_rs, o_ss, o_rs, s_ss, s_rs, a_ss, a_rs, r_ss, r_rs,
+    q_ss, q_rs, k_ss, k_rs, vv_ss, vv_rs, p_ss, p_rs, t_ss, t_rs,
+    o_ss, o_rs, s_ss, s_rs, a_ss, a_rs, f_ss, f_rs, r_ss, r_rs,
 ):
     me_s = lax.axis_index("seq")
     me_h = lax.axis_index("head")
@@ -205,139 +206,223 @@
         for copy in kv_copies(offset, head_from(offset)):
             copy.wait_recv()
 
-    def near(i, carry):
-        o, m = block(lax.rem(me_s + 1 + i, n_s), 0, half)
-        o_near[i] = o
-        m_near[i] = m
-        return carry
-
-    lax.fori_loop(0, n_s, near, 0)
+    n_a = n_s // 2
+    me_a, me_b = me_s // 2, lax.rem(me_s, 2)
+    pair = 2 * me_a + 1 - me_b
+
+    def major(j):
+        return lax.rem(me_a + 1 + j, n_a)
+
+    def near(j, carry):
+        first = block(2 * major(j) + 1 - me_b, 0, half)
+        second = block(2 * major(j) + me_b, 0, half)
+        o_near[j], m_near[j] = first
+        o_near[n_a + j], m_near[n_a + j] = second
+        return carry
+
+    lax.fori_loop(0, n_a, near, 0)
 
     for offset in range(half, n_h):
         for copy in kv_copies(offset, head_from(offset)):
             copy.wait_recv()
 
-    def o_copies(i, to, slot):
+    def p_copies(j):
         return (
             pltpu.make_async_remote_copy(
-                src_ref=o_send.at[i], dst_ref=o_recv.at[slot],
-                send_sem=o_ss.at[i], recv_sem=o_rs.at[i],
-                device_id=(to, me_h), device_id_type=MESH,
-            ),
-            pltpu.make_async_remote_copy(
-                src_ref=s_send.at[i], dst_ref=s_recv.at[slot],
-                send_sem=s_ss.at[i], recv_sem=s_rs.at[i],
-                device_id=(to, me_h), device_id_type=MESH,
-            ),
-        )
-
-    def far_block(i, u):
-        o2, m2 = block(u, half, n_h)
-        o1, m1 = o_near[i], m_near[i]
+                src_ref=p_send.at[j], dst_ref=p_recv.at[j],
+                send_sem=p_ss.at[j], recv_sem=p_rs.at[j],
+                device_id=(pair, me_h), device_id_type=MESH,
+            ),
+            pltpu.make_async_remote_copy(
+                src_ref=t_send.at[j], dst_ref=t_recv.at[j],
+                send_sem=t_ss.at[j], recv_sem=t_rs.at[j],
+                device_id=(pair, me_h), device_id_type=MESH,
+            ),
+        )
+
+    def o_copies(j, to_a, slot):
+        return (
+            pltpu.make_async_remote_copy(
+                src_ref=o_send.at[j], dst_ref=o_recv.at[slot],
+                send_sem=o_ss.at[j], recv_sem=o_rs.at[j],
+                device_id=(2 * to_a + me_b, me_h), device_id_type=MESH,
+            ),
+            pltpu.make_async_remote_copy(
+                src_ref=s_send.at[j], dst_ref=s_recv.at[slot],
+                send_sem=s_ss.at[j], recv_sem=s_rs.at[j],
+                device_id=(2 * to_a + me_b, me_h), device_id_type=MESH,
+            ),
+        )
+
+    def put_stats(ref, at, m, total):
+        m_rows, t_rows = to_rows(m, unit), to_rows(total, unit)
+        for r in range(n_rows):
+            ref[at, r : r + 1] = m_rows[r]
+            ref[at, n_rows + r : n_rows + r + 1] = t_rows[r]
+
+    def far_pair(j, carry):
+        o2, m2 = block(2 * major(j) + 1 - me_b, half, n_h)
+        o1, m1 = o_near[j], m_near[j]
         m = jnp.maximum(m1, m2)
         e1 = jnp.exp2((m1 - m) * scale)
         e2 = jnp.exp2((m2 - m) * scale)
-        numer = o1[:, :HD] * e1 + o2[:, :HD] * e2
-        total = o1[:, HD:] * e1 + o2[:, HD:] * e2
-        return numer.astype(BF16), to_rows(m, unit), to_rows(total, unit)
-
-    def far(i, carry):
-        u = lax.rem(me_s + 1 + i, n_s)
-        numer, m_rows, t_rows = far_block(i, u)
-        o_send[i] = numer
-        for r in range(n_rows):
-            s_send[i, r : r + 1] = m_rows[r]
-            s_send[i, n_rows + r : n_rows + r + 1] = t_rows[r]
-        for copy in o_copies(i, u, me_s):
+        p_send[j] = (o1[:, :HD] * e1 + o2[:, :HD] * e2).astype(BF16)
+        put_stats(t_send, j, m, o1[:, HD:] * e1 + o2[:, HD:] * e2)
+        for copy in p_copies(j):
             copy.start()
         return carry
 
-    lax.fori_loop(0, n_s - 1, far, 0)
-    numer, m_rows, t_rows = far_block(n_s - 1, me_s)
-    o_recv[me_s] = numer
-    for r in range(n_rows):
-        s_recv[me_s, r : r + 1] = m_rows[r]
-        s_recv[me_s, n_rows + r : n_rows + r + 1] = t_rows[r]
-
-    def o_wait(i, carry):
-        for copy in o_copies(i, lax.rem(me_s + 1 + i, n_s), lax.rem(me_s + n_s - 1 - i, n_s)):
+    lax.fori_loop(0, n_a, far_pair, 0)
+
+    def far_own(j):
+        o2, m2 = block(2 * major(j) + me_b, half, n_h)
+        for copy in p_copies(j):
             copy.wait_recv()
-        return carry
-
-    lax.fori_loop(0, n_s - 1, o_wait, 0)
+        o1, m1 = o_near[n_a + j], m_near[n_a + j]
+        m3 = to_col(t_recv[j, 0:n_rows], unit)
+        t3 = to_col(t_recv[j, n_rows : 2 * n_rows], unit)
+        m = jnp.maximum(jnp.maximum(m1, m2), m3)
+        e1 = jnp.exp2((m1 - m) * scale)
+        e2 = jnp.exp2((m2 - m) * scale)
+        e3 = jnp.exp2((m3 - m) * scale)
+        numer = o1[:, :HD] * e1 + o2[:, :HD] * e2 + p_recv[j].astype(F32) * e3
+        return numer.astype(BF16), m, o1[:, HD:] * e1 + o2[:, HD:] * e2 + t3 * e3
+
+    def far(j, carry):
+        numer, m, total = far_own(j)
+        o_send[j] = numer
+        put_stats(s_send, j, m, total)
+        for copy in o_copies(j, major(j), me_a):
+            copy.start()
+        return carry
+
+    lax.fori_loop(0, n_a - 1, far, 0)
+    numer, m, total = far_own(n_a - 1)
+    o_recv[me_a] = numer
+    put_stats(s_recv, me_a, m, total)
+
+    def o_wait(j, carry):
+        for copy in o_copies(j, major(j), lax.rem(me_a + n_a - 1 - j, n_a)):
+            copy.wait_recv()
+        return carry
+
+    lax.fori_loop(0, n_a - 1, o_wait, 0)
     m_all = s_recv[:, 0:n_rows]
     m_top = jnp.max(m_all, axis=0, keepdims=True)
     e_all = jnp.exp2((m_all - m_top) * scale)
     f_all = e_all / jnp.sum(e_all * s_recv[:, n_rows : 2 * n_rows], axis=0, keepdims=True)
     att = jnp.zeros((unit, HD), F32)
-    for b in range(n_s):
+    for b in range(n_a):
         att += to_col(f_all[b], unit) * o_recv[b].astype(F32)
-    a_send[...] = att.astype(BF16)
-
-    def place(u):
+
+    part = r_send.shape[2]
+    att = att.reshape(unit // (2 * part), 2, part, HD)
+    rows_here = unit // 2
+
+    def place(h, u):
         rows = (
-            pl.ds(0, unit)
+            pl.ds(0, rows_here)
             if per_head == 1
-            else pl.ds(pl.multiple_of(lax.rem(u, per_head) * unit, 16), unit)
-        )
-        return rows, pl.ds(pl.multiple_of((u // per_head) * HD, HD), HD)
-
-    def a_copy(i, to, u):
-        rows, cols = place(u)
+            else pl.ds(pl.multiple_of(lax.rem(u, per_head) * rows_here, 16), rows_here)
+        )
+        return h, rows, pl.ds(pl.multiple_of((u // per_head) * HD, HD), HD)
+
+    def a_copy(h, i, to, u):
         return pltpu.make_async_remote_copy(
-            src_ref=a_send, dst_ref=a_full.at[rows, cols],
-            send_sem=a_ss.at[i], recv_sem=a_rs.at[i],
+            src_ref=a_send.at[h], dst_ref=a_full.at[place(h, u)],
+            send_sem=a_ss.at[h, i], recv_sem=a_rs.at[h, i],
             device_id=(to, me_h), device_id_type=MESH,
         )
 
-    def a_start(i, carry):
-        a_copy(i, lax.rem(me_s + i, n_s), me_s).start()
-        return carry
-
-    def a_wait(i, carry):
-        a_copy(i, lax.rem(me_s + i, n_s), lax.rem(me_s + n_s - i, n_s)).wait_recv()
-        return carry
-
-    lax.fori_loop(1, n_s, a_start, 0)
-    rows, cols = place(me_s)
-    a_full[rows, cols] = a_send[...]
+    def f_copy(h, i, u):
+        return pltpu.make_async_remote_copy(
+            src_ref=a_full.at[place(h, u)], dst_ref=a_full.at[place(h, u)],
+            send_sem=f_ss.at[h, i], recv_sem=f_rs.at[h, i],
+            device_id=(pair, me_h), device_id_type=MESH,
+        )
+
+    def r_copy(h, offset, to):
+        return pltpu.make_async_remote_copy(
+            src_ref=r_send.at[h, to], dst_ref=r_recv.at[h, offset],
+            send_sem=r_ss.at[h, offset], recv_sem=r_rs.at[h, offset],
+            device_id=(me_s, to), device_id_type=MESH,
+        )
+
+    def ahead(i):
+        return 2 * lax.rem(me_a + i, n_a)
+
+    def behind(i):
+        return 2 * lax.rem(me_a + n_a - i, n_a)
+
+    for h in range(2):
+        a_send[h] = att[:, h].reshape(rows_here, HD).astype(BF16)
+
+        def a_start(i, carry, h=h):
+            a_copy(h, i, ahead(i) + me_b, me_s).start()
+            return carry
+
+        a_copy(h, 0, pair, me_s).start()
+        lax.fori_loop(1, n_a, a_start, 0)
+        a_full[place(h, me_s)] = a_send[h]
+
     load_out.wait()
-    lax.fori_loop(1, n_s, a_wait, 0)
-
-    share = jnp.dot(a_full[...], wobuf[...], preferred_element_type=F32)
-    r_send[...] = share.astype(BF16).reshape(r_send.shape)
-
-    def r_copy(offset, to):
-        return pltpu.make_async_remote_copy(
-            src_ref=r_send.at[to], dst_ref=r_recv.at[offset],
-            send_sem=r_ss.at[offset], recv_sem=r_rs.at[offset],
-            device_id=(me_s, to), device_id_type=MESH,
-        )
-
-    for offset in range(n_h - 1, 0, -1):
-        r_copy(offset, head_at(offset)).start()
-    total = r_send[me_h].astype(F32)
-    for offset in range(1, n_h):
-        r_copy(offset, head_from(offset)).wait_recv()
-        total += r_recv[offset].astype(F32)
-    out[...] = total.astype(BF16)
+    for h in range(2):
+
+        def forward(i, carry, h=h):
+            a_copy(h, i, ahead(i) + me_b, behind(i) + me_b).wait_recv()
+            f_copy(h, i, behind(i) + me_b).start()
+            return carry
+
+        def forwarded(i, carry, h=h):
+            f_copy(h, i, behind(i) + 1 - me_b).wait_recv()
+            return carry
+
+        lax.fori_loop(1, n_a, forward, 0)
+        a_copy(h, 0, pair, pair).wait_recv()
+        lax.fori_loop(1, n_a, forwarded, 0)
+        share = jnp.dot(a_full[h], wobuf[...], preferred_element_type=F32)
+        r_send[h] = share.astype(BF16).reshape(n_h, part, -1)
+        for offset in range(n_h - 1, 0, -1):
+            r_copy(h, offset, head_at(offset)).start()
+
+    for h in range(2):
+        total = r_send[h, me_h].astype(F32)
+        for offset in range(1, n_h):
+            r_copy(h, offset, head_from(offset)).wait_recv()
+            total += r_recv[h, offset].astype(F32)
+        out[h * part : (h + 1) * part] = total.astype(BF16)
 
     def q_sent(i, carry):
         q_copy(lax.rem(me_s + i, n_s), me_s, i).wait_send()
-        a_copy(i, lax.rem(me_s + i, n_s), me_s).wait_send()
-        return carry
-
-    def o_sent(i, carry):
-        for copy in o_copies(i, lax.rem(me_s + 1 + i, n_s), me_s):
+        return carry
+
+    def p_sent(j, carry):
+        for copy in p_copies(j):
             copy.wait_send()
         return carry
 
+    def o_sent(j, carry):
+        for copy in o_copies(j, major(j), me_a):
+            copy.wait_send()
+        return carry
+
     lax.fori_loop(1, n_s, q_sent, 0)
-    lax.fori_loop(0, n_s - 1, o_sent, 0)
+    lax.fori_loop(0, n_a, p_sent, 0)
+    lax.fori_loop(0, n_a - 1, o_sent, 0)
     for offset in range(1, n_h):
         for copy in kv_copies(offset, head_at(offset)):
             copy.wait_send()
-        r_copy(offset, head_at(offset)).wait_send()
+    for h in range(2):
+        a_copy(h, 0, pair, me_s).wait_send()
+
+        def a_sent(i, carry, h=h):
+            a_copy(h, i, ahead(i) + me_b, me_s).wait_send()
+            f_copy(h, i, behind(i) + me_b).wait_send()
+            return carry
+
+        lax.fori_loop(1, n_a, a_sent, 0)
+        for offset in range(1, n_h):
+            r_copy(h, offset, head_at(offset)).wait_send()
 
 
 def shards(n_s, n_h, vision, w_key, w_value, queries, w_out):
@@ -346,6 +431,7 @@
     heads = features // HD
     text = text_local * n_s
     unit = text_local * heads
+    n_a = n_s // 2
     out_cols = w_out.shape[1]
     n_c = max(d for d in range(1, 7) if width % (d * HD) == 0)
     k_c = width // n_c
@@ -363,20 +449,25 @@
         vmem((n_h, tokens, 2 * HD), BF16),
         vmem((n_s, unit, 2 * HD), F32),
         vmem((n_s, unit, HD), F32),
-        vmem((n_s, unit, HD), BF16),
-        vmem((n_s, 8, HD), F32),
-        vmem((n_s, unit, HD), BF16),
-        vmem((n_s, 8, HD), F32),
-        vmem((unit, HD), BF16),
-        vmem((text, features), BF16),
-        vmem((n_h, text // n_h, out_cols), BF16),
-        vmem((n_h, text // n_h, out_cols), BF16),
+        vmem((n_a, unit, HD), BF16),
+        vmem((n_a, 8, HD), F32),
+        vmem((n_a, unit, HD), BF16),
+        vmem((n_a, 8, HD), F32),
+        vmem((n_a, unit, HD), BF16),
+        vmem((n_a, 8, HD), F32),
+        vmem((n_a, unit, HD), BF16),
+        vmem((n_a, 8, HD), F32),
+        vmem((2, unit // 2, HD), BF16),
+        vmem((2, text // 2, features), BF16),
+        vmem((2, n_h, text // n_h // 2, out_cols), BF16),
+        vmem((2, n_h, text // n_h // 2, out_cols), BF16),
         dma((n_c,)), dma((n_h, n_c)), dma((n_h, n_c)), dma,
         dma((n_s,)), dma((n_s,)),
         dma((n_h,)), dma((n_h,)), dma((n_h,)), dma((n_h,)),
-        dma((n_s,)), dma((n_s,)), dma((n_s,)), dma((n_s,)),
-        dma((n_s,)), dma((n_s,)),
-        dma((n_h,)), dma((n_h,)),
+        dma((n_a,)), dma((n_a,)), dma((n_a,)), dma((n_a,)),
+        dma((n_a,)), dma((n_a,)), dma((n_a,)), dma((n_a,)),
+        dma((2, n_a)), dma((2, n_a)), dma((2, n_a)), dma((2, n_a)),
+        dma((2, n_h)), dma((2, n_h)),
     ]
     anywhere = pl.BlockSpec(memory_space=pl.ANY)
     inside = pl.BlockSpec(memory_space=pltpu.VMEM)

time: 66.4 us -> 59 us (0.89)
  the two profiles are of different devices: /device:TPU:28 before, /device:TPU:0 now
where the time goes in v2:
time: 59 us; the launch traced here: 58.8 us
  Pallas kernels  57.2 us (97%)
  local copies, waits for them, and re-layouts  1.57 us (3%)
    pallas_call x1, Pallas kernels, shards(): pl.pallas_call(functools.partial(kernel, n_s, n_h, n_c), out_shape=jax.Sh...  57.2 us
    unnamed x1, local copies, waits for them, and re-layouts  1.57 us

profile of v2, /device:TPU:0, one launch (start us, length us, event | category | flops | bytes accessed | tf_op | source)
XLA Modules:
  0.0 58.8 jit_solution(17503074829086763216)
XLA Ops:
  0.0 57.2 %shard_map.55 = bf16[64,1024]{1,0:T(8,128)(2,1)} custom-call(bf16[512,7680]{1,0:T(8,128)(2,1)} %vision.1, bf16[7680,512]{1,0:T(8,128)(2,1)} %w_key.1, bf16[7680,512]{1,0:T(8,128)(2,1)} %w_value.1, bf16[32,1024]{1,0:T(8,128)(2,1)} %q.1, bf16[1024,1024]{1,0:T(8,128)(2,1)} %w_out.1), custom_call_target="tpu_custom_call" | custom-call | tf_op jit(solution)/shard_map/pallas_call | solution.py:474
  57.2 1.6 %copy.7 = bf16[64,1024]{1,0:T(8,128)(2,1)} copy(bf16[64,1024]{1,0:T(8,128)(2,1)} %shard_map.55) | data formatting | bytes 262144
